TPU v7x, 32 devices: a whole 2x2x4 slice. The times are simulated.
32 devices in a mesh: mesh: 2 (over y), seq: 4 (over x, core), fsdp: 4 (over z).
Axes of the slice: x: 2, y: 2, z: 4, core: 2. Of those that a mesh axis runs over, the one named last changes fastest.
Arguments:
- latents: bfloat16 [4, 512, 5120], P('fsdp', 'mesh'), may hold values from -8 to 8
- noise: bfloat16 [4, 512, 5120], P('fsdp', 'mesh'), may hold values from -6 to 6
- noise_level: float32 [4], P('fsdp'), may hold values from 0.05 to 0.3
- group_index: int32 [4, 512], P('fsdp'), may hold values from 0 to 7, never falling along the last dimension, each value on 1 to 128 neighbouring positions
- projections: bfloat16 [2, 5120, 3, 3072], P('mesh', 'fsdp', None, 'seq'), may hold values from -1 to 1, as said below
- upstream: bfloat16 [4, 512, 3072], P('fsdp', None, 'seq'), may hold values from -0.29882812 to 0.29882812
Outputs:
- direction: bfloat16 [4, 512, 3072], P('fsdp', ('mesh', 'seq'))
- fake_grads: float32 [5120, 3, 3072], P(('mesh', 'fsdp'), None, 'seq')
Inputs may be any that keep to these rules, and one draw needn't show every extreme that they name: `projections`: along the third dimension: query, key and value projection, in that order. `group_index`: along each clip the group numbers never fall; each of the 8 groups holds 1 to 128 tokens.
All inputs are finite; a program needn't handle non-finite values.
Results may differ from a plain program's by a relative error of at most 0.018.
Values may be sent and summed in bfloat16 or wider, within the bound.
No kernel may reach another device: no remote copies, remote signals or barrier semaphores. Data moves between devices by JAX's collectives and lax.ppermute only.
A program may use at most 128 MiB of HBM per device.

v0:
```python
import math

import jax
import jax.numpy as jnp
from jax import lax
from jax.sharding import PartitionSpec as P

HEAD = 128


def shifted(value, axis, by):
    devices = lax.axis_size(axis)
    pairs = [(i, i + by) for i in range(devices) if 0 <= i + by < devices]
    return lax.ppermute(value, axis, pairs)


def softmax_parts(queries, key_rows, visible, score_scale):
    scores = (
        jnp.einsum("qhd,khd->hqk", queries, key_rows, preferred_element_type=jnp.float32)
        * score_scale
    )
    scores = jnp.where(visible[None], scores, jnp.float32(-1e30))
    highest = jnp.max(scores, axis=-1, keepdims=True)
    weights = jnp.exp(scores - highest)
    return weights / jnp.sum(weights, axis=-1, keepdims=True)


def contract(columns, factors):
    return lax.dot_general(
        columns, factors, (((0,), (0,)), ((), ())), preferred_element_type=jnp.float32
    )


def per_device(latents, noise, noise_level, group_index, projections, upstream):
    model_index = lax.axis_index("mesh")
    clip_rows, clip_noise = (
        lax.all_gather(latents[0], "mesh", axis=0, tiled=True),
        lax.all_gather(noise[0], "mesh", axis=0, tiled=True),
    )
    noise_rate = noise_level[0]
    noised = (
        (1.0 - noise_rate) * clip_rows.astype(jnp.float32)
        + noise_rate * clip_noise.astype(jnp.float32)
    ).astype(jnp.bfloat16)
    length = noised.shape[0]
    head_cols = projections.shape[3]
    head_size = HEAD
    local_heads = head_cols // head_size
    triple_width = 3 * head_cols
    weight_piece = lax.all_gather(projections, "fsdp", axis=1, tiled=True)
    row_count = weight_piece.shape[1]
    columns = noised
    projected = jnp.dot(
        columns, weight_piece.reshape(row_count, triple_width), preferred_element_type=jnp.float32
    )
    triple = projected.astype(jnp.bfloat16).reshape(length, 3, local_heads, head_size)
    queries = triple[:, 0]
    key_rows = triple[:, 1]
    values = triple[:, 2]
    groups = group_index[0]
    visible = groups[None, :] <= groups[:, None]
    score_scale = 1.0 / math.sqrt(head_size)
    probabilities = softmax_parts(queries, key_rows, visible, score_scale)
    prob_low = probabilities.astype(jnp.bfloat16)
    attended = jnp.einsum("hqk,khd->qhd", prob_low, values, preferred_element_type=jnp.float32)
    attended = attended.astype(jnp.bfloat16).reshape(length, head_cols)
    model_sign = jnp.where(model_index == 1, 1.0, -1.0).astype(jnp.float32)
    paired = lax.psum_scatter(
        (model_sign * attended.astype(jnp.float32)).astype(jnp.bfloat16),
        "mesh",
        scatter_dimension=0,
        tiled=True,
    )
    direction = lax.all_to_all(paired, "seq", split_axis=0, concat_axis=1, tiled=True)
    grad_out = upstream[0].reshape(length, local_heads, head_size)
    value_grad = jnp.einsum(
        "hqk,qhd->khd", prob_low, grad_out, preferred_element_type=jnp.float32
    ).astype(jnp.bfloat16)
    prob_grad = jnp.einsum("qhd,khd->hqk", grad_out, values, preferred_element_type=jnp.float32)
    row_inner = jnp.sum(probabilities * prob_grad, axis=-1, keepdims=True)
    score_grad = (probabilities * (prob_grad - row_inner) * score_scale).astype(jnp.bfloat16)
    query_grad = jnp.einsum(
        "hqk,khd->qhd", score_grad, key_rows, preferred_element_type=jnp.float32
    ).astype(jnp.bfloat16)
    key_grad = jnp.einsum(
        "hqk,qhd->khd", score_grad, queries, preferred_element_type=jnp.float32
    ).astype(jnp.bfloat16)
    cotangents = jnp.stack([query_grad, key_grad, value_grad], axis=1).reshape(length, triple_width)
    shard_rows = projections.shape[1] // lax.axis_size("mesh")
    received = shifted(cotangents, "mesh", -1)
    fake_side = jnp.where(model_index == 1, cotangents, received)
    offset = model_index * (noised.shape[1] // lax.axis_size("mesh"))
    columns = lax.dynamic_slice_in_dim(noised, offset, lax.axis_size("fsdp") * shard_rows, 1)
    summed = lax.psum_scatter(
        contract(columns, fake_side).astype(jnp.bfloat16), "fsdp", scatter_dimension=0, tiled=True
    ).astype(jnp.float32)
    return (direction[None], summed.reshape(shard_rows, 3, head_cols))


def solution(mesh):
    in_specs = (
        P("fsdp", "mesh", None),
        P("fsdp", "mesh", None),
        P("fsdp"),
        P("fsdp", None),
        P("mesh", "fsdp", None, "seq"),
        P("fsdp", None, "seq"),
    )
    out_specs = (P("fsdp", ("mesh", "seq"), None), P(("mesh", "fsdp"), None, "seq"))
    return jax.shard_map(
        per_device, mesh=mesh, in_specs=in_specs, out_specs=out_specs, check_vma=False
    )
```

profile of v0, /device:TPU:0, one launch (start us, length us, event | category | flops | bytes accessed | tf_op | source)
XLA Modules:
  0.0 903.1 jit_solution(1102400297052748517)
XLA Ops:
  7.2 0.0 all-gather.10.cloned.1.call-start
  7.2 0.7 all-gather.10.cloned.1.call-update
  7.9 0.0 all-gather.8.cloned.1.call-start
  7.9 0.7 all-gather.8.cloned.1.call-update
  8.6 0.0 copy-start.2
  8.7 0.0 all-gather.6.cloned.1.call-start
  8.7 9.0 copy.38
  17.7 0.0 copy-start.3
  17.7 0.0 all-gather.6.cloned.1.call-update
  17.7 0.0 reduce-scatter.3.cloned.1.call-start
  18.4 0.0 copy-done.2
  18.4 0.3 copy.45
  18.7 0.0 copy-done.3
  18.7 0.2 broadcast_compare_fusion
  18.9 61.9 %all-gather.10.cloned.1.call-done = bf16[1,512,5120]{2,1,0:T(8,128)(2,1)} async-done(((bf16[1,256,5120]{2,1,0:T(8,128)(2,1)}), bf16[1,512,5120]{2,1,0:T(8,128)(2,1)}) %all-gather.10.cloned.1.call-update) | async-done | bytes 5242896 | tf_op jit(solution)/shard_map/all_gather | solution.py:38
  80.8 70.1 %all-gather.8.cloned.1.call-done = bf16[1,512,5120]{2,1,0:T(8,128)(2,1)} async-done(((bf16[1,256,5120]{2,1,0:T(8,128)(2,1)}), bf16[1,512,5120]{2,1,0:T(8,128)(2,1)}) %all-gather.8.cloned.1.call-update) | async-done | bytes 5242896 | tf_op jit(solution)/shard_map/all_gather | solution.py:37
  151.0 8.5 add_convert_fusion
  159.5 393.3 %all-gather.6.cloned.1.call-done = bf16[1,5120,3,768]{1,3,2,0:T(8,128)(2,1)} async-done(((bf16[1,1280,3,768]{1,3,2,0:T(8,128)(2,1)}), bf16[1,5120,3,768]{1,3,2,0:T(8,128)(2,1)}) %all-gather.6.cloned.1.call-update) | async-done | bytes 23592976 | tf_op jit(solution)/shard_map/all_gather | solution.py:50
  552.8 18.4 %fusion.8 = bf16[512,2304]{1,0:T(8,128)(2,1)} fusion(bf16[5120,2304]{0,1:T(8,128)(2,1)} %bitcast.103, bf16[1,512,5120]{2,1,0:T(8,128)(2,1)} %add_convert_fusion), kind=kOutput, calls=%fused_computation.14 | convolution fusion | flops 12080775168 | bytes 31195136 | tf_op jit(solution)/shard_map/dot_general | solution.py:53
  571.2 2.8 copy.39
  574.1 1.0 fusion.41
  575.1 3.7 fusion.40
  578.8 4.6 fusion.49
  583.3 11.9 %fusion.39 = bf16[512,1,6,128]{0,3,2,1:T(8,128)(2,1)} fusion(f32[6,512,512]{2,1,0:T(8,128)} %fusion.40, bf16[512,3,6,128]{0,3,2,1:T(8,128)(2,1)S(1)} %bitcast.94, f32[6,512,512]{1,2,0:T(8,128)} %get-tuple-element.9, f32[6,512]{1,0:T(8,128)S(1)} %get-tuple-element.8), kind=kOutput, calls=%fused_computation.38 | convolution fusion | flops 414060032 | bytes 26771456 | tf_op jit(solution)/shard_map/hqk,khd->qhd/dot_general | solution.py:82
  595.2 10.4 %fusion.38 = bf16[512,1,6,128]{0,3,2,1:T(8,128)(2,1)} fusion(f32[6,512,512]{2,1,0:T(8,128)} %fusion.40, bf16[512,3,6,128]{0,3,2,1:T(8,128)(2,1)S(1)} %bitcast.95, f32[6,512,512]{1,2,0:T(8,128)} %get-tuple-element.9, f32[6,512]{1,0:T(8,128)S(1)} %get-tuple-element.8), kind=kOutput, calls=%fused_computation.37 | convolution fusion | flops 414060032 | bytes 26771456 | tf_op jit(solution)/shard_map/hqk,qhd->khd/dot_general | solution.py:85
  605.6 0.0 copy-start
  605.6 0.0 copy-start.1
  605.6 4.1 fusion.33
  609.7 0.0 copy-done
  609.7 0.0 copy-done.1
  609.7 1.7 pad_maximum_fusion
  611.3 1.5 collective-permute-start
  612.8 3.4 multiply_convert_fusion
  616.3 1.1 copy.43
  617.4 0.0 reduce-scatter.3.cloned.1.call-update
  617.5 0.0 reduce-scatter.5.cloned.1.call-start
  617.5 57.6 %collective-permute-done = bf16[512,2304]{0,1:T(8,128)(2,1)} collective-permute-done((bf16[512,2304]{0,1:T(8,128)(2,1)}, bf16[512,2304]{0,1:T(8,128)(2,1)}, u32[]{:S(2)}, u32[]{:S(2)}) %collective-permute-start) | collective-permute-done | bytes 2359328 | tf_op jit(solution)/shard_map/ppermute | solution.py:14
  675.2 11.3 %convolution_convert_fusion = bf16[2560,2304]{1,0:T(8,128)(2,1)} fusion(bf16[1,512,5120]{2,1,0:T(8,128)(2,1)} %add_convert_fusion, s32[]{:T(128)S(6)} %select_n.21, bf16[512,2304]{0,1:T(8,128)(2,1)} %bitcast.21, bf16[512,2304]{0,1:T(8,128)(2,1)} %collective-permute-done, pred[]{:T(512)S(6)} %eq.4), kind=kOutput, calls=%fused_computation.2 | convolution fusion | flops 6046875648 | bytes 19136516 | tf_op jit(solution)/shard_map/dot_general | solution.py:29
  686.4 0.0 reduce-scatter.5.cloned.1.call-update
  686.4 0.0 reduce-scatter.3.cloned.1.call-done
  686.5 10.9 %all_to_all.16 = bf16[4,64,768]{2,1,0:T(8,128)(2,1)S(1)} all-to-all(bf16[4,64,768]{2,1,0:T(8,128)(2,1)} %bitcast.101), channel_id=1, replica_groups=mesh['mesh'=2,'seq'=4,'fsdp'=4] {'seq'}, dimensions={0} | all-to-all | bytes 786432 | tf_op jit(solution)/shard_map/all_to_all | solution.py:74
  697.4 0.3 copy.44
  697.7 1.0 broadcast_in_dim.21
  698.7 184.3 %reduce-scatter.5.cloned.1.call-done = bf16[640,2304]{1,0:T(8,128)(2,1)} async-done(((bf16[2560,2304]{1,0:T(8,128)(2,1)}), bf16[640,2304]{1,0:T(8,128)(2,1)}) %reduce-scatter.5.cloned.1.call-update) | async-done | bytes 2949136 | tf_op jit(solution)/shard_map/reduce_scatter | solution.py:94
  883.0 5.9 copy.53
  888.9 7.7 copy.54
Async XLA Ops:
  7.2 73.7 %all-gather.10.cloned.1.call-start = ((), (), s32[]{:S(2)}) async-start(), calls=%async_computation.7 | async-start | bytes 7864320 | tf_op jit(solution)/shard_map/all_gather | solution.py:38
  7.9 143.1 %all-gather.8.cloned.1.call-start = ((), (), s32[]{:S(2)}) async-start(), calls=%async_computation.6 | async-start | bytes 7864320 | tf_op jit(solution)/shard_map/all_gather | solution.py:37
  8.6 9.8 %copy-start.2 = (bf16[1,512,768]{2,1,0:T(8,128)(2,1)S(1)}, bf16[1,512,768]{2,1,0:T(8,128)(2,1)}, u32[]{:S(2)}) copy-start(bf16[1,512,768]{2,1,0:T(8,128)(2,1)} %param.11) | copy-start | bytes 2359300
  8.7 544.1 %all-gather.6.cloned.1.call-start = ((), (), s32[]{:S(2)}) async-start(), calls=%async_computation.3 | async-start | bytes 29491200 | tf_op jit(solution)/shard_map/all_gather | solution.py:50
  17.7 1.0 copy-start.3
  17.7 668.8 %reduce-scatter.3.cloned.1.call-start = ((), (), s32[]{:S(2)}) async-start(), calls=%async_computation.4 | async-start | bytes 1179648 | tf_op jit(solution)/shard_map/reduce_scatter | solution.py:68
  605.6 4.1 copy-start
  605.6 4.1 copy-start.1
  611.3 63.8 %collective-permute-start = (bf16[512,2304]{0,1:T(8,128)(2,1)}, bf16[512,2304]{0,1:T(8,128)(2,1)}, u32[]{:S(2)}, u32[]{:S(2)}) collective-permute-start(bf16[512,2304]{0,1:T(8,128)(2,1)} %bitcast.21), channel_id=1, source_target_pairs={{16,0},{17,1},{18,2},{19,3},{20,4},{21,5},{22,6},{23,7},{24,8},{25... | collective-permute-start | bytes 7077896 | tf_op jit(solution)/shard_map/ppermute | solution.py:14
  617.5 265.5 %reduce-scatter.5.cloned.1.call-start = ((), (), s32[]{:S(2)}) async-start(), calls=%async_computation.5 | async-start | bytes 14745600 | tf_op jit(solution)/shard_map/reduce_scatter | solution.py:94
Sparse Core Ops, SparseCore 0:
  9.5 71.2 all-gather.9
  82.4 68.5 all-gather.7
  153.1 399.6 all-gather.5
  617.6 26.6 reduce-scatter.2
  686.6 196.3 reduce-scatter.4
where the time goes:
time: 904 us; the launch traced here: 903 us
  waiting for transfers between devices  769 us (85%)
  matrix products  64.1 us (7%)
  local copies, waits for them, and re-layouts  28.1 us (3%)
  other arithmetic  15 us (2%)
  between operations  14.5 us (2%)
  blocking collectives  10.9 us (1%)
    all_gather x1, waiting for transfers between devices, per_device(): weight_piece = lax.all_gather(projections, 'fsdp', axis=1, tiled=True)  393 us
    reduce_scatter x1, waiting for transfers between devices, per_device(): lax.psum_scatter(contract(columns, fake_side).astype(jnp.bfloat16), 'fsdp...  184 us
    all_gather x1, waiting for transfers between devices, per_device(): lax.all_gather(latents[0], 'mesh', axis=0, tiled=True)  70.1 us
    all_gather x1, waiting for transfers between devices, per_device(): lax.all_gather(noise[0], 'mesh', axis=0, tiled=True)  61.9 us
    ppermute x1, waiting for transfers between devices, shifted(): return lax.ppermute(value, axis, pairs)  57.6 us
    dot_general x1, matrix products, per_device(): jnp.dot(columns, weight_piece.reshape(row_count, triple_width), preferred...  18.4 us
  transfers between devices with their start and end apart: 6, of which 5 were waited for; matrix products, arithmetic and copies ran while one was open for 4% of the time, Pallas kernels for 0%

commit v1 on v0

v1 whole, which is shorter than its diff:
```python
import math

import jax
import jax.numpy as jnp
from jax import lax
from jax.sharding import PartitionSpec as P

HEAD = 128


def contract(columns, factors):
    return lax.dot_general(
        columns, factors, (((0,), (0,)), ((), ())), preferred_element_type=jnp.float32
    )


def in_order(relative, index):
    size = relative.shape[0]
    doubled = jnp.concatenate([relative, relative], axis=0)
    return lax.dynamic_slice_in_dim(doubled, size - index, size, 0)


def spread_mesh(value):
    size = lax.axis_size("mesh")
    pieces = [value]
    for d in range(1, size):
        pairs = [((i + d) % size, i) for i in range(size)]
        pieces.append(lax.ppermute(value, "mesh", pairs))
    return in_order(jnp.stack(pieces), lax.axis_index("mesh"))


def spread_seq(value, cores, over_cores):
    size = lax.axis_size("seq")
    chips = size // cores
    index = lax.axis_index("seq")
    steps = cores if over_cores else chips
    pieces = [value]
    for d in range(1, steps):
        pairs = []
        for i in range(size):
            chip, core = divmod(i, cores)
            if over_cores:
                source = chip * cores + (core + d) % cores
            else:
                source = (chip + d) % chips * cores + core
            pairs.append((source, i))
        pieces.append(lax.ppermute(value, "seq", pairs))
    place = index % cores if over_cores else index // cores
    return in_order(jnp.stack(pieces), place)


def plane_gather(value, cores):
    first = spread_seq(spread_mesh(value[0]), cores, False)
    second = spread_mesh(spread_seq(value[1], cores, False))
    first = jnp.swapaxes(first, 0, 1)
    both = spread_seq(jnp.stack([first, second]), cores, True)
    both = jnp.transpose(both, (1, 4, 2, 3, 0, 5, 6))
    _, clips, mesh, chips, _, rows, width = both.shape
    return both.reshape(2, clips, mesh * chips * cores * rows, width)


def softmax(queries, key_rows, visible, score_scale):
    scores = (
        jnp.einsum("cqd,ckd->cqk", queries, key_rows, preferred_element_type=jnp.float32)
        * score_scale
    )
    scores = jnp.where(visible, scores, jnp.float32(-1e30))
    highest = jnp.max(scores, axis=-1, keepdims=True)
    weights = jnp.exp(scores - highest)
    return weights / jnp.sum(weights, axis=-1, keepdims=True)


def attention(teacher, fake, grad_out, visible, score_scale):
    def parts(triple):
        return triple[..., :HEAD], triple[..., HEAD : 2 * HEAD], triple[..., 2 * HEAD :]

    queries, key_rows, values = parts(teacher)
    prob_low = softmax(queries, key_rows, visible, score_scale).astype(jnp.bfloat16)
    teacher_out = jnp.einsum(
        "cqk,ckd->cqd", prob_low, values, preferred_element_type=jnp.float32
    ).astype(jnp.bfloat16)
    queries, key_rows, values = parts(fake)
    probabilities = softmax(queries, key_rows, visible, score_scale)
    prob_low = probabilities.astype(jnp.bfloat16)
    fake_out = jnp.einsum(
        "cqk,ckd->cqd", prob_low, values, preferred_element_type=jnp.float32
    ).astype(jnp.bfloat16)
    direction = (fake_out.astype(jnp.float32) - teacher_out.astype(jnp.float32)).astype(
        jnp.bfloat16
    )
    value_grad = jnp.einsum("cqk,cqd->ckd", prob_low, grad_out, preferred_element_type=jnp.float32)
    prob_grad = jnp.einsum("cqd,ckd->cqk", grad_out, values, preferred_element_type=jnp.float32)
    row_inner = jnp.sum(probabilities * prob_grad, axis=-1, keepdims=True)
    score_grad = (probabilities * (prob_grad - row_inner) * score_scale).astype(jnp.bfloat16)
    query_grad = jnp.einsum(
        "cqk,ckd->cqd", score_grad, key_rows, preferred_element_type=jnp.float32
    )
    key_grad = jnp.einsum("cqk,cqd->ckd", score_grad, queries, preferred_element_type=jnp.float32)
    cotangents = jnp.concatenate([query_grad, key_grad, value_grad], axis=-1)
    return direction, cotangents.astype(jnp.bfloat16)


def per_device(latents, noise, noise_level, group_index, projections, upstream):
    planes = lax.axis_size("fsdp")
    sides = lax.axis_size("mesh")
    lanes = lax.axis_size("seq")
    plane = lax.axis_index("fsdp")
    side = lax.axis_index("mesh")
    lane = lax.axis_index("seq")
    half = planes // 2
    cores = 2 if lanes % 2 == 0 else 1
    low_half = plane < half
    first_side = side == 0
    swap = [(0, 1), (1, 0)]

    rows, _, head_cols = projections.shape[1:]
    width = latents.shape[2]
    length = group_index.shape[1]
    heads = head_cols // HEAD
    pairs = (heads + 1) // 2
    score_scale = 1.0 / math.sqrt(HEAD)

    def by_distance(stacked):
        low, high = stacked[:half], stacked[::-1][:half]
        return jnp.stack([jnp.where(low_half, low, high), jnp.where(low_half, high, low)])

    piece = latents.shape[1] // lanes
    own_rows = lax.dynamic_slice_in_dim(latents[0], lane * piece, piece, 0)
    own_noise = lax.dynamic_slice_in_dim(noise[0], lane * piece, piece, 0)
    noise_rate = noise_level[0]
    noised = (
        (1.0 - noise_rate) * own_rows.astype(jnp.float32)
        + noise_rate * own_noise.astype(jnp.float32)
    ).astype(jnp.bfloat16)

    def tokens_of(blocks):
        clips = lax.all_to_all(blocks, "fsdp", split_axis=0, concat_axis=0, tiled=True)
        return plane_gather(by_distance(clips), cores)

    tokens = tokens_of(jnp.swapaxes(noised.reshape(piece, planes, rows), 0, 1))
    near = tokens[0].reshape(half * length, rows)
    far = tokens[1].reshape(half * length, rows)

    finals = []
    for head in range(heads):
        factors = projections[0, :, :, head * HEAD : (head + 1) * HEAD].reshape(rows, 3 * HEAD)
        far_part = jnp.dot(far, factors, preferred_element_type=jnp.float32)
        near_part = jnp.dot(near, factors, preferred_element_type=jnp.float32)
        running = far_part.astype(jnp.bfloat16)
        for hop in range(1, planes):
            hops = [(hop - 1, hop), (planes - hop, planes - 1 - hop)]
            arrived = lax.ppermute(running, "fsdp", hops).astype(jnp.float32)
            part = far_part if hop < half else near_part
            running = (arrived + part).astype(jnp.bfloat16)
        finals.append(running.reshape(half, length, 3 * HEAD))

    groups = by_distance(lax.all_gather(group_index, "fsdp", axis=0, tiled=True))[0]
    visible = groups[:, None, :] <= groups[:, :, None]
    kept_heads = [jnp.minimum(2 * j + side, heads - 1) for j in range(pairs)]
    own_up = jnp.stack(
        [lax.dynamic_slice_in_dim(upstream[0], h * HEAD, HEAD, 1) for h in kept_heads]
    )
    ups = [own_up]
    for k in range(1, half):
        ups.append(lax.ppermute(own_up, "fsdp", [(k, 0), (planes - 1 - k, planes - 1)]))
    ups = jnp.stack(ups, axis=1)

    shard_rows = rows // sides
    columns = tokens_of(
        jnp.transpose(noised.reshape(piece, sides, planes, shard_rows), (2, 0, 1, 3)).reshape(
            planes, piece, rows
        )
    )
    near_columns = columns[0].reshape(half * length, rows)
    far_columns = columns[1].reshape(half * length, rows)
    outer = (plane == 0) | (plane == planes - 1)
    distance = jnp.minimum(plane, planes - 1 - plane)

    def pick(hops_of):
        picked = hops_of[half - 1]
        for d in range(half - 2, -1, -1):
            picked = jnp.where(distance == d, hops_of[d], picked)
        return picked

    directions, grads = [], []
    for j in range(pairs):
        even, odd = finals[2 * j], finals[min(2 * j + 1, heads - 1)]
        kept = jnp.where(first_side, even, odd)
        swapped = lax.ppermute(jnp.where(first_side, odd, even), "mesh", swap)
        teacher = jnp.where(first_side, kept, swapped)
        fake = jnp.where(first_side, swapped, kept)
        direction, cotangents = attention(teacher, fake, ups[j], visible, score_scale)
        directions.append(direction)
        passed = [cotangents]
        for hop in range(1, planes):
            hops = [(hop - 1, hop), (planes - hop, planes - 1 - hop)]
            passed.append(lax.ppermute(passed[-1], "fsdp", hops))
        near_cot = pick(passed[:half]).reshape(half * length, 3 * HEAD)
        far_cot = pick(passed[::-1][:half]).reshape(half * length, 3 * HEAD)
        grad = contract(near_columns, near_cot) + contract(far_columns, far_cot)
        grad = grad.reshape(sides, shard_rows, 3, 1, HEAD)
        own_grad = jnp.where(first_side, grad[0], grad[1])
        sent = jnp.where(first_side, grad[1], grad[0]).astype(jnp.bfloat16)
        other = lax.ppermute(sent, "mesh", swap).astype(jnp.float32)
        grads.append(jnp.where(first_side, own_grad, other))
        grads.append(jnp.where(first_side, other, own_grad))
    summed = jnp.concatenate(grads[:heads], axis=2).reshape(shard_rows, 3, head_cols)

    directions = jnp.stack(directions, axis=2)
    local = directions[0]
    for k in range(1, half):
        moved = lax.ppermute(directions[k], "fsdp", [(0, k), (planes - 1, planes - 1 - k)])
        local = jnp.where(distance == k, moved, local)
    local = lax.all_to_all(
        local.reshape(length, pairs * HEAD), ("mesh", "seq"), split_axis=0, concat_axis=1, tiled=True
    )
    local = local.reshape(-1, sides, lanes, pairs, HEAD)
    local = jnp.transpose(local, (0, 2, 3, 1, 4)).reshape(-1, lanes, pairs * sides, HEAD)
    direction = local[:, :, :heads].reshape(1, -1, lanes * head_cols)
    return (direction, summed)


def solution(mesh):
    in_specs = (
        P("fsdp", "mesh", None),
        P("fsdp", "mesh", None),
        P("fsdp"),
        P("fsdp", None),
        P("mesh", "fsdp", None, "seq"),
        P("fsdp", None, "seq"),
    )
    out_specs = (P("fsdp", ("mesh", "seq"), None), P(("mesh", "fsdp"), None, "seq"))
    return jax.shard_map(
        per_device, mesh=mesh, in_specs=in_specs, out_specs=out_specs, check_vma=False
    )
```

time: 904 us -> 589 us (0.65)
  waiting for transfers between devices: 769 us -> 283 us
  starting transfers between devices: 1.7 us -> 81.8 us
  matrix products: 64.1 us -> 104 us
  other arithmetic: 15 us -> 45.4 us
  local copies, waits for them, and re-layouts: 28.1 us -> 52.1 us
  between operations: 14.5 us -> 2.59 us
    all_gather x3 -> x0, waiting for transfers between devices: 525 us -> none  [the longest x1 393 us: per_device(): weight_piece = lax.all_gather(projections, 'fsdp', axis=1, tiled=True)]
    ppermute x1 -> x45, waiting for transfers between devices: 57.6 us -> 266 us  [the longest x18 172 us: per_device(): arrived = lax.ppermute(running, 'fsdp', hops).astype(jnp.float32)]
    reduce_scatter x2 -> x0, waiting for transfers between devices: 184 us -> none  [the longest x1 184 us: per_device(): lax.psum_scatter(contract(columns, fake_side).astype(jnp.bfloat16), 'fsdp...]
    ppermute x1 -> x45, starting transfers between devices: 1.5 us -> 67.9 us  [the longest x18 26.3 us: per_device(): arrived = lax.ppermute(running, 'fsdp', hops).astype(jnp.float32)]
    dot_general x7 -> x30, matrix products: 52.8 us -> 73 us  [the longest x6 15.7 us: attention(): jnp.einsum('cqk,ckd->cqd', prob_low, values, preferred_element_type=jnp.f...]
    all_to_all x0 -> x3, waiting for transfers between devices: none -> 17 us  [the longest x2 15 us: tokens_of(): lax.all_to_all(blocks, 'fsdp', split_axis=0, concat_axis=0, tiled=True)]
    select_n x0 -> x18, other arithmetic: none -> 14.9 us  [the longest x3 5.76 us: per_device(): fake = jnp.where(first_side, swapped, kept)]
    all_gather x0 -> x1, blocking collectives: none -> 14.9 us  [per_device(): lax.all_gather(group_index, 'fsdp', axis=0, tiled=True)]
  transfers between devices with their start and end apart: 6 -> 48, of which waited for: 5 -> 27; matrix products, arithmetic and copies ran while one was open for 4% -> 31% of each run, Pallas kernels for 0% -> 0%
where the time goes in v1:
time: 589 us; the launch traced here: 583 us
  waiting for transfers between devices  283 us (48%)
  matrix products  104 us (18%)
  starting transfers between devices  81.8 us (14%)
  local copies, waits for them, and re-layouts  52.1 us (9%)
  other arithmetic  45.4 us (8%)
  blocking collectives  14.9 us (3%)
    ppermute x18, waiting for transfers between devices, per_device(): arrived = lax.ppermute(running, 'fsdp', hops).astype(jnp.float32)  172 us
    ppermute x9, waiting for transfers between devices, per_device(): passed.append(lax.ppermute(passed[-1], 'fsdp', hops))  40 us
    ppermute x6, waiting for transfers between devices, spread_seq(): pieces.append(lax.ppermute(value, 'seq', pairs))  27.1 us
    ppermute x18, starting transfers between devices, per_device(): arrived = lax.ppermute(running, 'fsdp', hops).astype(jnp.float32)  26.3 us
    unnamed x74, local copies, waits for them, and re-layouts  25.3 us
    dot_general x6, matrix products, contract(): lax.dot_general(columns, factors, (((0,), (0,)), ((), ())), preferred_ele...  19.7 us
    ppermute x3, waiting for transfers between devices, per_device(): other = lax.ppermute(sent, 'mesh', swap).astype(jnp.float32)  17.7 us
    ppermute x9, starting transfers between devices, per_device(): passed.append(lax.ppermute(passed[-1], 'fsdp', hops))  16 us
  transfers between devices with their start and end apart: 48, of which 27 were waited for; matrix products, arithmetic and copies ran while one was open for 31% of the time, Pallas kernels for 0%

profile of v1, /device:TPU:0, one launch (start us, length us, event | category | flops | bytes accessed | tf_op | source)
XLA Modules:
  0.0 583.4 jit_solution(2219725365836542020)
XLA Ops:
  4.2 6.3 %all-to-all-start = ((bf16[4,64,1280]{2,1,0:T(8,128)(2,1)}), bf16[4,64,1280]{2,1,0:T(8,128)(2,1)S(1)}, u32[]{:S(2)}, u32[]{:S(2)}) async-start(bf16[4,64,1280]{2,1,0:T(8,128)(2,1)} %copy.152), calls=%async_computation | async-start | bytes 1310720 | tf_op jit(solution)/shard_map/all_to_all | solution.py:137
  12.8 15.0 %all-to-all-done = bf16[4,64,1280]{2,1,0:T(8,128)(2,1)S(1)} async-done(((bf16[4,64,1280]{2,1,0:T(8,128)(2,1)}), bf16[4,64,1280]{2,1,0:T(8,128)(2,1)S(1)}, u32[]{:S(2)}, u32[]{:S(2)}) %all-to-all-start) | async-done | bytes 655392 | tf_op jit(solution)/shard_map/all_to_all | solution.py:137
  27.8 4.2 all-to-all-start.2
  33.7 5.4 fusion.387
  39.2 14.9 %all-gather = s32[4,1,512]{2,1,0:T(1,128)S(1)} all-gather(s32[1,1,512]{2,1,0:T(1,128)S(1)} %bitcast.251), channel_id=1, replica_groups=mesh['mesh'=2,'seq'=4,'fsdp'=4] {'fsdp'}, dimensions={0}, use_global_device_ids=true | all-gather | bytes 10240 | tf_op jit(solution)/shard_map/all_gather | solution.py:157
  56.6 8.1 %collective-permute-done.2 = bf16[2,64,1280]{2,1,0:T(8,128)(2,1)S(1)} collective-permute-done((bf16[2,64,1280]{2,1,0:T(8,128)(2,1)S(1)}, bf16[2,64,1280]{2,1,0:T(8,128)(2,1)S(1)}, u32[]{:S(2)}, u32[]{:S(2)}) %collective-permute-start.2) | collective-permute-done | bytes 327712 | tf_op jit(solution)/shard_map/ppermute | solution.py:47
  67.7 7.1 %collective-permute-done.1 = bf16[2,2,64,1280]{3,2,1,0:T(8,128)(2,1)S(1)} collective-permute-done((bf16[2,2,64,1280]{3,2,1,0:T(8,128)(2,1)S(1)}, bf16[2,2,64,1280]{3,2,1,0:T(8,128)(2,1)S(1)}, u32[]{:S(2)}, u32[]{:S(2)}) %collective-permute-start.1) | collective-permute-done | bytes 655392 | tf_op jit(solution)/shard_map/ppermute | solution.py:47
  98.5 6.3 %collective-permute-done.27 = bf16[2,64,1280]{2,1,0:T(8,128)(2,1)S(1)} collective-permute-done((bf16[2,64,1280]{2,1,0:T(8,128)(2,1)S(1)}, bf16[2,64,1280]{2,1,0:T(8,128)(2,1)S(1)}, u32[]{:S(2)}, u32[]{:S(2)}) %collective-permute-start.27) | collective-permute-done | bytes 327712 | tf_op jit(solution)/shard_map/ppermute | solution.py:28
  109.8 11.9 %collective-permute-done.28 = bf16[2,2,64,1280]{3,2,1,0:T(8,128)(2,1)S(1)} collective-permute-done((bf16[2,2,64,1280]{3,2,1,0:T(8,128)(2,1)S(1)}, bf16[2,2,64,1280]{3,2,1,0:T(8,128)(2,1)S(1)}, u32[]{:S(2)}, u32[]{:S(2)}) %collective-permute-start.28) | collective-permute-done | bytes 655392 | tf_op jit(solution)/shard_map/ppermute | solution.py:47
  124.4 6.2 %fusion.16 = bf16[2,2,2,2,2,64,1280]{6,5,1,3,2,0,4:T(8,128)(2,1)S(1)} fusion(s32[]{:T(128)S(6)} %select_n.325, bf16[1,2,2,2,2,64,1280]{6,5,4,3,2,1,0:T(8,128)(2,1)S(1)} %get-tuple-element.27, bf16[1,2,2,2,2,64,1280]{6,5,4,3,2,1,0:T(8,128)(2,1)} %bitcast.16), kind=kLoop, calls=%fused_computation.24 | loop fusion | flops 7864320 | bytes 10485764 | tf_op jit(solution)/shard_map/transpose | solution.py:57
  156.5 7.6 %collective-permute-done.15 = bf16[1024,384]{1,0:T(8,128)(2,1)S(1)} collective-permute-done((bf16[1024,384]{1,0:T(8,128)(2,1)S(1)}, bf16[1024,384]{1,0:T(8,128)(2,1)S(1)}, u32[]{:S(2)}, u32[]{:S(2)}) %collective-permute-start.15) | collective-permute-done | bytes 786464 | tf_op jit(solution)/shard_map/ppermute | solution.py:152
  164.2 4.4 collective-permute-start.8
  168.8 12.2 %collective-permute-done.12 = bf16[1024,384]{1,0:T(8,128)(2,1)S(1)} collective-permute-done((bf16[1024,384]{1,0:T(8,128)(2,1)S(1)}, bf16[1024,384]{1,0:T(8,128)(2,1)S(1)}, u32[]{:S(2)}, u32[]{:S(2)}) %collective-permute-start.12) | collective-permute-done | bytes 786464 | tf_op jit(solution)/shard_map/ppermute | solution.py:152
  181.0 4.6 collective-permute-start.5
  185.8 12.1 %collective-permute-done.22 = bf16[1024,384]{1,0:T(8,128)(2,1)S(1)} collective-permute-done((bf16[1024,384]{1,0:T(8,128)(2,1)S(1)}, bf16[1024,384]{1,0:T(8,128)(2,1)S(1)}, u32[]{:S(2)}, u32[]{:S(2)}) %collective-permute-start.22) | collective-permute-done | bytes 786464 | tf_op jit(solution)/shard_map/ppermute | solution.py:152
  198.8 15.9 %collective-permute-done.19 = bf16[1024,384]{1,0:T(8,128)(2,1)S(1)} collective-permute-done((bf16[1024,384]{1,0:T(8,128)(2,1)S(1)}, bf16[1024,384]{1,0:T(8,128)(2,1)S(1)}, u32[]{:S(2)}, u32[]{:S(2)}) %collective-permute-start.19) | collective-permute-done | bytes 786464 | tf_op jit(solution)/shard_map/ppermute | solution.py:152
  215.6 15.9 %collective-permute-done.8 = bf16[1024,384]{1,0:T(8,128)(2,1)S(1)} collective-permute-done((bf16[1024,384]{1,0:T(8,128)(2,1)S(1)}, bf16[1024,384]{1,0:T(8,128)(2,1)S(1)}, u32[]{:S(2)}, u32[]{:S(2)}) %collective-permute-start.8) | collective-permute-done | bytes 786464 | tf_op jit(solution)/shard_map/ppermute | solution.py:152
  232.5 15.7 %collective-permute-done.5 = bf16[1024,384]{1,0:T(8,128)(2,1)S(1)} collective-permute-done((bf16[1024,384]{1,0:T(8,128)(2,1)S(1)}, bf16[1024,384]{1,0:T(8,128)(2,1)S(1)}, u32[]{:S(2)}, u32[]{:S(2)}) %collective-permute-start.5) | collective-permute-done | bytes 786464 | tf_op jit(solution)/shard_map/ppermute | solution.py:152
  257.0 22.2 %collective-permute-done.17 = bf16[1024,384]{1,0:T(8,128)(2,1)S(1)} collective-permute-done((bf16[1024,384]{1,0:T(8,128)(2,1)S(1)}, bf16[1024,384]{1,0:T(8,128)(2,1)S(1)}, u32[]{:S(2)}, u32[]{:S(2)}) %collective-permute-start.17) | collective-permute-done | bytes 786464 | tf_op jit(solution)/shard_map/ppermute | solution.py:152
  280.5 15.6 %collective-permute-done.14 = bf16[1024,384]{1,0:T(8,128)(2,1)S(1)} collective-permute-done((bf16[1024,384]{1,0:T(8,128)(2,1)S(1)}, bf16[1024,384]{1,0:T(8,128)(2,1)S(1)}, u32[]{:S(2)}, u32[]{:S(2)}) %collective-permute-start.14) | collective-permute-done | bytes 786464 | tf_op jit(solution)/shard_map/ppermute | solution.py:152
  299.4 4.8 fusion.12
  304.2 8.7 %collective-permute-done.24 = bf16[1024,384]{1,0:T(8,128)(2,1)S(1)} collective-permute-done((bf16[1024,384]{1,0:T(8,128)(2,1)S(1)}, bf16[1024,384]{1,0:T(8,128)(2,1)S(1)}, u32[]{:S(2)}, u32[]{:S(2)}) %collective-permute-start.24) | collective-permute-done | bytes 786464 | tf_op jit(solution)/shard_map/ppermute | solution.py:152
  314.2 15.6 %collective-permute-done.21 = bf16[1024,384]{1,0:T(8,128)(2,1)S(1)} collective-permute-done((bf16[1024,384]{1,0:T(8,128)(2,1)S(1)}, bf16[1024,384]{1,0:T(8,128)(2,1)S(1)}, u32[]{:S(2)}, u32[]{:S(2)}) %collective-permute-start.21) | collective-permute-done | bytes 786464 | tf_op jit(solution)/shard_map/ppermute | solution.py:152
  332.7 13.9 %collective-permute-done.10 = bf16[1024,384]{1,0:T(8,128)(2,1)S(1)} collective-permute-done((bf16[1024,384]{1,0:T(8,128)(2,1)S(1)}, bf16[1024,384]{1,0:T(8,128)(2,1)S(1)}, u32[]{:S(2)}, u32[]{:S(2)}) %collective-permute-start.10) | collective-permute-done | bytes 786464 | tf_op jit(solution)/shard_map/ppermute | solution.py:152
  346.6 16.9 %collective-permute-done.7 = bf16[1024,384]{1,0:T(8,128)(2,1)S(1)} collective-permute-done((bf16[1024,384]{1,0:T(8,128)(2,1)S(1)}, bf16[1024,384]{1,0:T(8,128)(2,1)S(1)}, u32[]{:S(2)}, u32[]{:S(2)}) %collective-permute-start.7) | collective-permute-done | bytes 786464 | tf_op jit(solution)/shard_map/ppermute | solution.py:152
  372.9 5.1 fusion.72
  378.0 5.2 fusion.75
  385.7 3.3 fusion.398
  392.6 5.1 fusion.66
  397.7 5.2 fusion.69
  418.8 3.3 fusion.87
  425.2 3.2 fusion.97
  439.6 4.4 fusion.78
  445.2 4.5 fusion.81
  455.4 3.5 all-to-all-start.1
  458.8 2.9 fusion.388
  475.6 4.6 fusion.434
  486.8 3.6 fusion.433
  492.0 17.5 %collective-permute-done.39 = bf16[2,512,384]{1,2,0:T(8,128)(2,1)} collective-permute-done((bf16[2,512,384]{1,2,0:T(8,128)(2,1)}, bf16[2,512,384]{1,2,0:T(8,128)(2,1)}, u32[]{:S(2)}, u32[]{:S(2)}) %collective-permute-start.39) | collective-permute-done | bytes 786464 | tf_op jit(solution)/shard_map/ppermute | solution.py:197
  510.7 15.6 %collective-permute-done.43 = bf16[2,512,384]{1,2,0:T(8,128)(2,1)} collective-permute-done((bf16[2,512,384]{1,2,0:T(8,128)(2,1)}, bf16[2,512,384]{1,2,0:T(8,128)(2,1)}, u32[]{:S(2)}, u32[]{:S(2)}) %collective-permute-start.43) | collective-permute-done | bytes 786464 | tf_op jit(solution)/shard_map/ppermute | solution.py:197
  529.1 3.6 convolution_add_fusion.1
  533.6 2.9 collective-permute-start.40
  536.4 6.8 %collective-permute-done.35 = bf16[2,512,384]{1,2,0:T(8,128)(2,1)} collective-permute-done((bf16[2,512,384]{1,2,0:T(8,128)(2,1)}, bf16[2,512,384]{1,2,0:T(8,128)(2,1)}, u32[]{:S(2)}, u32[]{:S(2)}) %collective-permute-start.35) | collective-permute-done | bytes 786464 | tf_op jit(solution)/shard_map/ppermute | solution.py:197
  545.6 4.0 convolution_add_fusion.2
  549.7 2.9 collective-permute-start.36
  554.6 10.2 %collective-permute-done.36 = bf16[640,3,1,128]{0,3,2,1:T(8,128)(2,1)S(1)} collective-permute-done((bf16[640,3,1,128]{0,3,2,1:T(8,128)(2,1)S(1)}, bf16[640,3,1,128]{0,3,2,1:T(8,128)(2,1)S(1)}, u32[]{:S(2)}, u32[]{:S(2)}) %collective-permute-start.36) | collective-permute-done | bytes 491552 | tf_op jit(solution)/shard_map/ppermute | solution.py:204
  565.2 7.5 %collective-permute-done.44 = bf16[640,3,1,128]{0,3,2,1:T(8,128)(2,1)S(1)} collective-permute-done((bf16[640,3,1,128]{0,3,2,1:T(8,128)(2,1)S(1)}, bf16[640,3,1,128]{0,3,2,1:T(8,128)(2,1)S(1)}, u32[]{:S(2)}, u32[]{:S(2)}) %collective-permute-start.44) | collective-permute-done | bytes 491552 | tf_op jit(solution)/shard_map/ppermute | solution.py:204
  575.5 7.7 %copy.209 = f32[640,3,768]{2,0,1:T(8,128)} copy(f32[640,3,768]{0,2,1:T(8,128)} %bitcast.176) | data formatting | bytes 11796480
  (255 shorter events, 176.5 us)
Async XLA Ops:
  4.2 23.6 %all-to-all-start = ((bf16[4,64,1280]{2,1,0:T(8,128)(2,1)}), bf16[4,64,1280]{2,1,0:T(8,128)(2,1)S(1)}, u32[]{:S(2)}, u32[]{:S(2)}) async-start(bf16[4,64,1280]{2,1,0:T(8,128)(2,1)} %copy.152), calls=%async_computation | async-start | bytes 1310720 | tf_op jit(solution)/shard_map/all_to_all | solution.py:137
  27.8 64.7 %all-to-all-start.2 = ((bf16[4,64,1280]{2,1,0:T(8,128)(2,1)}), bf16[4,64,1280]{2,1,0:T(8,128)(2,1)}, u32[]{:S(2)}, u32[]{:S(2)}) async-start(bf16[4,64,1280]{2,1,0:T(8,128)(2,1)} %reshape.275), calls=%async_computation.2 | async-start | bytes 1310720 | tf_op jit(solution)/shard_map/all_to_all | solution.py:137
  32.1 23.4 %collective-permute-start = (bf16[2,64,1280]{2,1,0:T(8,128)(2,1)S(1)}, bf16[2,64,1280]{2,1,0:T(8,128)(2,1)S(1)}, u32[]{:S(2)}, u32[]{:S(2)}) collective-permute-start(bf16[2,64,1280]{2,1,0:T(8,128)(2,1)S(1)} %get-tuple-element.36), channel_id=1, source_target_pairs={{16,0},{0,16},{17,1},{1,17},{18,2},{2,18},{19,3},{3,19},{20,4},{4,... | collective-permute-start | bytes 983048 | tf_op jit(solution)/shard_map/ppermute | solution.py:28
  54.1 10.6 %collective-permute-start.2 = (bf16[2,64,1280]{2,1,0:T(8,128)(2,1)S(1)}, bf16[2,64,1280]{2,1,0:T(8,128)(2,1)S(1)}, u32[]{:S(2)}, u32[]{:S(2)}) collective-permute-start(bf16[2,64,1280]{2,1,0:T(8,128)(2,1)S(1)} %get-tuple-element.37), channel_id=1, source_target_pairs={{8,0},{12,4},{0,8},{4,12},{9,1},{13,5},{1,9},{5,13},{10,2},{14,6},... | collective-permute-start | bytes 983048 | tf_op jit(solution)/shard_map/ppermute | solution.py:47
  56.0 18.8 %collective-permute-start.1 = (bf16[2,2,64,1280]{3,2,1,0:T(8,128)(2,1)S(1)}, bf16[2,2,64,1280]{3,2,1,0:T(8,128)(2,1)S(1)}, u32[]{:S(2)}, u32[]{:S(2)}) collective-permute-start(bf16[2,2,64,1280]{3,2,1,0:T(8,128)(2,1)S(1)} %fusion.146), channel_id=1, source_target_pairs={{8,0},{12,4},{0,8},{4,12},{9,1},{13,5},{1,9},{5,13},{10,2},{14,6},... | collective-permute-start | bytes 1966088 | tf_op jit(solution)/shard_map/ppermute | solution.py:47
  65.2 10.7 %collective-permute-start.3 = (bf16[2,2,64,1280]{3,2,1,0:T(8,128)(2,1)S(1)}, bf16[2,2,64,1280]{3,2,1,0:T(8,128)(2,1)S(1)}, u32[]{:S(2)}, u32[]{:S(2)}) collective-permute-start(bf16[2,2,64,1280]{3,2,1,0:T(8,128)(2,1)S(1)} %fusion.143), channel_id=1, source_target_pairs={{16,0},{0,16},{17,1},{1,17},{18,2},{2,18},{19,3},{3,19},{20,4},{4,... | collective-permute-start | bytes 1966088 | tf_op jit(solution)/shard_map/ppermute | solution.py:28
  78.6 45.8 %collective-permute-start.4 = (bf16[2,2,2,2,64,1280]{5,4,3,2,1,0:T(8,128)(2,1)}, bf16[2,2,2,2,64,1280]{5,4,3,2,1,0:T(8,128)(2,1)}, u32[]{:S(2)}, u32[]{:S(2)}) collective-permute-start(bf16[2,2,2,2,64,1280]{5,4,3,2,1,0:T(8,128)(2,1)} %get-tuple-element.26), channel_id=1, source_target_pairs={{4,0},{0,4},{12,8},{8,12},{5,1},{1,5},{13,9},{9,13},{6,2},{2,6},{1... | collective-permute-start | bytes 7864328 | tf_op jit(solution)/shard_map/ppermute | solution.py:47
  94.6 10.2 %collective-permute-start.27 = (bf16[2,64,1280]{2,1,0:T(8,128)(2,1)S(1)}, bf16[2,64,1280]{2,1,0:T(8,128)(2,1)S(1)}, u32[]{:S(2)}, u32[]{:S(2)}) collective-permute-start(bf16[2,64,1280]{2,1,0:T(8,128)(2,1)S(1)} %get-tuple-element.34), channel_id=1, source_target_pairs={{16,0},{0,16},{17,1},{1,17},{18,2},{2,18},{19,3},{3,19},{20,4},{4,... | collective-permute-start | bytes 983048 | tf_op jit(solution)/shard_map/ppermute | solution.py:28
  96.2 10.6 %collective-permute-start.29 = (bf16[2,64,1280]{2,1,0:T(8,128)(2,1)S(1)}, bf16[2,64,1280]{2,1,0:T(8,128)(2,1)S(1)}, u32[]{:S(2)}, u32[]{:S(2)}) collective-permute-start(bf16[2,64,1280]{2,1,0:T(8,128)(2,1)S(1)} %get-tuple-element.35), channel_id=1, source_target_pairs={{8,0},{12,4},{0,8},{4,12},{9,1},{13,5},{1,9},{5,13},{10,2},{14,6},... | collective-permute-start | bytes 983048 | tf_op jit(solution)/shard_map/ppermute | solution.py:47
  105.3 16.4 %collective-permute-start.28 = (bf16[2,2,64,1280]{3,2,1,0:T(8,128)(2,1)S(1)}, bf16[2,2,64,1280]{3,2,1,0:T(8,128)(2,1)S(1)}, u32[]{:S(2)}, u32[]{:S(2)}) collective-permute-start(bf16[2,2,64,1280]{3,2,1,0:T(8,128)(2,1)S(1)} %fusion.140), channel_id=1, source_target_pairs={{8,0},{12,4},{0,8},{4,12},{9,1},{13,5},{1,9},{5,13},{10,2},{14,6},... | collective-permute-start | bytes 1966088 | tf_op jit(solution)/shard_map/ppermute | solution.py:47
  107.3 16.1 %collective-permute-start.30 = (bf16[2,2,64,1280]{3,2,1,0:T(8,128)(2,1)S(1)}, bf16[2,2,64,1280]{3,2,1,0:T(8,128)(2,1)S(1)}, u32[]{:S(2)}, u32[]{:S(2)}) collective-permute-start(bf16[2,2,64,1280]{3,2,1,0:T(8,128)(2,1)S(1)} %fusion.137), channel_id=1, source_target_pairs={{16,0},{0,16},{17,1},{1,17},{18,2},{2,18},{19,3},{3,19},{20,4},{4,... | collective-permute-start | bytes 1966088 | tf_op jit(solution)/shard_map/ppermute | solution.py:28
  124.3 173.5 %collective-permute-start.31 = (bf16[2,2,2,2,64,1280]{5,4,3,1,2,0:T(8,128)(2,1)S(1)}, bf16[2,2,2,2,64,1280]{5,4,3,1,2,0:T(8,128)(2,1)S(1)}, u32[]{:S(2)}, u32[]{:S(2)}) collective-permute-start(bf16[2,2,2,2,64,1280]{5,4,3,1,2,0:T(8,128)(2,1)S(1)} %get-tuple-element.24), channel_id=1, source_target_pairs={{4,0},{0,4},{12,8},{8,12},{5,1},{1,5},{13,9},{9,13},{6,2},{2,6},{1... | collective-permute-start | bytes 7864328 | tf_op jit(solution)/shard_map/ppermute | solution.py:47
  144.9 19.2 %collective-permute-start.15 = (bf16[1024,384]{1,0:T(8,128)(2,1)S(1)}, bf16[1024,384]{1,0:T(8,128)(2,1)S(1)}, u32[]{:S(2)}, u32[]{:S(2)}) collective-permute-start(bf16[1024,384]{1,0:T(8,128)(2,1)S(1)} %get-tuple-element.53), channel_id=1, source_target_pairs={{0,1},{3,2},{4,5},{7,6},{8,9},{11,10},{12,13},{15,14},{16,17},{19,... | collective-permute-start | bytes 2359304 | tf_op jit(solution)/shard_map/ppermute | solution.py:152
  149.4 31.6 %collective-permute-start.12 = (bf16[1024,384]{1,0:T(8,128)(2,1)S(1)}, bf16[1024,384]{1,0:T(8,128)(2,1)S(1)}, u32[]{:S(2)}, u32[]{:S(2)}) collective-permute-start(bf16[1024,384]{1,0:T(8,128)(2,1)S(1)} %get-tuple-element.51), channel_id=1, source_target_pairs={{0,1},{3,2},{4,5},{7,6},{8,9},{11,10},{12,13},{15,14},{16,17},{19,... | collective-permute-start | bytes 2359304 | tf_op jit(solution)/shard_map/ppermute | solution.py:152
  150.7 47.1 %collective-permute-start.22 = (bf16[1024,384]{1,0:T(8,128)(2,1)S(1)}, bf16[1024,384]{1,0:T(8,128)(2,1)S(1)}, u32[]{:S(2)}, u32[]{:S(2)}) collective-permute-start(bf16[1024,384]{1,0:T(8,128)(2,1)S(1)} %get-tuple-element.47), channel_id=1, source_target_pairs={{0,1},{3,2},{4,5},{7,6},{8,9},{11,10},{12,13},{15,14},{16,17},{19,... | collective-permute-start | bytes 2359304 | tf_op jit(solution)/shard_map/ppermute | solution.py:152
  155.2 59.5 %collective-permute-start.19 = (bf16[1024,384]{1,0:T(8,128)(2,1)S(1)}, bf16[1024,384]{1,0:T(8,128)(2,1)S(1)}, u32[]{:S(2)}, u32[]{:S(2)}) collective-permute-start(bf16[1024,384]{1,0:T(8,128)(2,1)S(1)} %get-tuple-element.45), channel_id=1, source_target_pairs={{0,1},{3,2},{4,5},{7,6},{8,9},{11,10},{12,13},{15,14},{16,17},{19,... | collective-permute-start | bytes 2359304 | tf_op jit(solution)/shard_map/ppermute | solution.py:152
  164.2 67.4 %collective-permute-start.8 = (bf16[1024,384]{1,0:T(8,128)(2,1)S(1)}, bf16[1024,384]{1,0:T(8,128)(2,1)S(1)}, u32[]{:S(2)}, u32[]{:S(2)}) collective-permute-start(bf16[1024,384]{1,0:T(8,128)(2,1)S(1)} %get-tuple-element.59), channel_id=1, source_target_pairs={{0,1},{3,2},{4,5},{7,6},{8,9},{11,10},{12,13},{15,14},{16,17},{19,... | collective-permute-start | bytes 2359304 | tf_op jit(solution)/shard_map/ppermute | solution.py:152
  181.0 67.2 %collective-permute-start.5 = (bf16[1024,384]{1,0:T(8,128)(2,1)S(1)}, bf16[1024,384]{1,0:T(8,128)(2,1)S(1)}, u32[]{:S(2)}, u32[]{:S(2)}) collective-permute-start(bf16[1024,384]{1,0:T(8,128)(2,1)S(1)} %get-tuple-element.57), channel_id=1, source_target_pairs={{0,1},{3,2},{4,5},{7,6},{8,9},{11,10},{12,13},{15,14},{16,17},{19,... | collective-permute-start | bytes 2359304 | tf_op jit(solution)/shard_map/ppermute | solution.py:152
  197.9 51.3 %collective-permute-start.16 = (bf16[1024,384]{1,0:T(8,128)(2,1)S(1)}, bf16[1024,384]{1,0:T(8,128)(2,1)S(1)}, u32[]{:S(2)}, u32[]{:S(2)}) collective-permute-start(bf16[1024,384]{1,0:T(8,128)(2,1)S(1)} %add_convert_fusion.8), channel_id=1, source_target_pairs={{1,2},{2,1},{5,6},{6,5},{9,10},{10,9},{13,14},{14,13},{17,18},{18,... | collective-permute-start | bytes 2359304 | tf_op jit(solution)/shard_map/ppermute | solution.py:152
  214.7 35.3 %collective-permute-start.13 = (bf16[1024,384]{1,0:T(8,128)(2,1)S(1)}, bf16[1024,384]{1,0:T(8,128)(2,1)S(1)}, u32[]{:S(2)}, u32[]{:S(2)}) collective-permute-start(bf16[1024,384]{1,0:T(8,128)(2,1)S(1)} %add_convert_fusion.11), channel_id=1, source_target_pairs={{1,2},{2,1},{5,6},{6,5},{9,10},{10,9},{13,14},{14,13},{17,18},{18,... | collective-permute-start | bytes 2359304 | tf_op jit(solution)/shard_map/ppermute | solution.py:152
  231.6 19.4 %collective-permute-start.23 = (bf16[1024,384]{1,0:T(8,128)(2,1)S(1)}, bf16[1024,384]{1,0:T(8,128)(2,1)S(1)}, u32[]{:S(2)}, u32[]{:S(2)}) collective-permute-start(bf16[1024,384]{1,0:T(8,128)(2,1)S(1)} %add_convert_fusion.2), channel_id=1, source_target_pairs={{1,2},{2,1},{5,6},{6,5},{9,10},{10,9},{13,14},{14,13},{17,18},{18,... | collective-permute-start | bytes 2359304 | tf_op jit(solution)/shard_map/ppermute | solution.py:152
  248.2 4.3 collective-permute-start.20
  249.1 4.8 collective-permute-start.9
  250.0 5.5 collective-permute-start.6
  250.9 28.3 %collective-permute-start.17 = (bf16[1024,384]{1,0:T(8,128)(2,1)S(1)}, bf16[1024,384]{1,0:T(8,128)(2,1)S(1)}, u32[]{:S(2)}, u32[]{:S(2)}) collective-permute-start(bf16[1024,384]{1,0:T(8,128)(2,1)S(1)} %add_convert_fusion.7), channel_id=1, source_target_pairs={{2,3},{1,0},{6,7},{5,4},{10,11},{9,8},{14,15},{13,12},{18,19},{17,... | collective-permute-start | bytes 2359304 | tf_op jit(solution)/shard_map/ppermute | solution.py:152
  252.5 43.6 %collective-permute-start.14 = (bf16[1024,384]{1,0:T(8,128)(2,1)S(1)}, bf16[1024,384]{1,0:T(8,128)(2,1)S(1)}, u32[]{:S(2)}, u32[]{:S(2)}) collective-permute-start(bf16[1024,384]{1,0:T(8,128)(2,1)S(1)} %add_convert_fusion.10), channel_id=1, source_target_pairs={{2,3},{1,0},{6,7},{5,4},{10,11},{9,8},{14,15},{13,12},{18,19},{17,... | collective-permute-start | bytes 2359304 | tf_op jit(solution)/shard_map/ppermute | solution.py:152
  254.0 59.0 %collective-permute-start.24 = (bf16[1024,384]{1,0:T(8,128)(2,1)S(1)}, bf16[1024,384]{1,0:T(8,128)(2,1)S(1)}, u32[]{:S(2)}, u32[]{:S(2)}) collective-permute-start(bf16[1024,384]{1,0:T(8,128)(2,1)S(1)} %add_convert_fusion.1), channel_id=1, source_target_pairs={{2,3},{1,0},{6,7},{5,4},{10,11},{9,8},{14,15},{13,12},{18,19},{17,... | collective-permute-start | bytes 2359304 | tf_op jit(solution)/shard_map/ppermute | solution.py:152
  255.5 74.3 %collective-permute-start.21 = (bf16[1024,384]{1,0:T(8,128)(2,1)S(1)}, bf16[1024,384]{1,0:T(8,128)(2,1)S(1)}, u32[]{:S(2)}, u32[]{:S(2)}) collective-permute-start(bf16[1024,384]{1,0:T(8,128)(2,1)S(1)} %add_convert_fusion.4), channel_id=1, source_target_pairs={{2,3},{1,0},{6,7},{5,4},{10,11},{9,8},{14,15},{13,12},{18,19},{17,... | collective-permute-start | bytes 2359304 | tf_op jit(solution)/shard_map/ppermute | solution.py:152
  279.2 67.4 %collective-permute-start.10 = (bf16[1024,384]{1,0:T(8,128)(2,1)S(1)}, bf16[1024,384]{1,0:T(8,128)(2,1)S(1)}, u32[]{:S(2)}, u32[]{:S(2)}) collective-permute-start(bf16[1024,384]{1,0:T(8,128)(2,1)S(1)} %add_convert_fusion.13), channel_id=1, source_target_pairs={{2,3},{1,0},{6,7},{5,4},{10,11},{9,8},{14,15},{13,12},{18,19},{17,... | collective-permute-start | bytes 2359304 | tf_op jit(solution)/shard_map/ppermute | solution.py:152
  296.1 67.4 %collective-permute-start.7 = (bf16[1024,384]{1,0:T(8,128)(2,1)S(1)}, bf16[1024,384]{1,0:T(8,128)(2,1)S(1)}, u32[]{:S(2)}, u32[]{:S(2)}) collective-permute-start(bf16[1024,384]{1,0:T(8,128)(2,1)S(1)} %add_convert_fusion.16), channel_id=1, source_target_pairs={{2,3},{1,0},{6,7},{5,4},{10,11},{9,8},{14,15},{13,12},{18,19},{17,... | collective-permute-start | bytes 2359304 | tf_op jit(solution)/shard_map/ppermute | solution.py:152
  297.8 68.6 %collective-permute-start.18 = (bf16[2,512,384]{2,1,0:T(8,128)(2,1)S(1)}, bf16[2,512,384]{2,1,0:T(8,128)(2,1)S(1)}, u32[]{:S(2)}, u32[]{:S(2)}) collective-permute-start(bf16[2,512,384]{2,1,0:T(8,128)(2,1)S(1)} %bitcast.237), channel_id=1, source_target_pairs={{0,16},{16,0},{1,17},{17,1},{2,18},{18,2},{3,19},{19,3},{4,20},{20... | collective-permute-start | bytes 2359304 | tf_op jit(solution)/shard_map/ppermute | solution.py:189
  312.9 57.1 %collective-permute-start.32 = (bf16[3,512,128]{2,1,0:T(8,128)(2,1)}, bf16[3,512,128]{2,1,0:T(8,128)(2,1)S(1)}, u32[]{:S(2)}, u32[]{:S(2)}) collective-permute-start(bf16[3,512,128]{2,1,0:T(8,128)(2,1)} %get-tuple-element.41), channel_id=1, source_target_pairs={{1,0},{2,3},{5,4},{6,7},{9,8},{10,11},{13,12},{14,15},{17,16},{18,... | collective-permute-start | bytes 1179656 | tf_op jit(solution)/shard_map/ppermute | solution.py:165
  331.2 52.0 %collective-permute-start.25 = (bf16[2,512,384]{2,1,0:T(8,128)(2,1)}, bf16[2,512,384]{2,1,0:T(8,128)(2,1)}, u32[]{:S(2)}, u32[]{:S(2)}) collective-permute-start(bf16[2,512,384]{2,1,0:T(8,128)(2,1)} %bitcast.32), channel_id=1, source_target_pairs={{0,16},{16,0},{1,17},{17,1},{2,18},{18,2},{3,19},{19,3},{4,20},{20... | collective-permute-start | bytes 2359304 | tf_op jit(solution)/shard_map/ppermute | solution.py:189
  364.9 38.0 %collective-permute-start.11 = (bf16[2,512,384]{2,1,0:T(8,128)(2,1)}, bf16[2,512,384]{2,1,0:T(8,128)(2,1)}, u32[]{:S(2)}, u32[]{:S(2)}) collective-permute-start(bf16[2,512,384]{2,1,0:T(8,128)(2,1)} %bitcast.22), channel_id=1, source_target_pairs={{0,16},{16,0},{1,17},{17,1},{2,18},{18,2},{3,19},{19,3},{4,20},{20... | collective-permute-start | bytes 2359304 | tf_op jit(solution)/shard_map/ppermute | solution.py:189
  410.0 58.9 %collective-permute-start.37 = (bf16[2,512,384]{1,2,0:T(8,128)(2,1)}, bf16[2,512,384]{1,2,0:T(8,128)(2,1)}, u32[]{:S(2)}, u32[]{:S(2)}) collective-permute-start(bf16[2,512,384]{1,2,0:T(8,128)(2,1)} %pad_maximum_fusion.4), channel_id=1, source_target_pairs={{0,1},{3,2},{4,5},{7,6},{8,9},{11,10},{12,13},{15,14},{16,17},{19,... | collective-permute-start | bytes 2359304 | tf_op jit(solution)/shard_map/ppermute | solution.py:197
  414.4 56.0 %collective-permute-start.41 = (bf16[2,512,384]{1,2,0:T(8,128)(2,1)}, bf16[2,512,384]{1,2,0:T(8,128)(2,1)}, u32[]{:S(2)}, u32[]{:S(2)}) collective-permute-start(bf16[2,512,384]{1,2,0:T(8,128)(2,1)} %pad_maximum_fusion.5), channel_id=1, source_target_pairs={{0,1},{3,2},{4,5},{7,6},{8,9},{11,10},{12,13},{15,14},{16,17},{19,... | collective-permute-start | bytes 2359304 | tf_op jit(solution)/shard_map/ppermute | solution.py:197
  437.4 16.5 %collective-permute-start.26 = (bf16[512,3,128]{2,0,1:T(8,128)(2,1)}, bf16[512,3,128]{2,0,1:T(8,128)(2,1)}, u32[]{:S(2)}, u32[]{:S(2)}) collective-permute-start(bf16[512,3,128]{2,0,1:T(8,128)(2,1)} %slice_bitcast_fusion.1), channel_id=1, source_target_pairs={{0,1},{3,2},{4,5},{7,6},{8,9},{11,10},{12,13},{15,14},{16,17},{19,... | collective-permute-start | bytes 1179656 | tf_op jit(solution)/shard_map/ppermute | solution.py:212
  450.8 23.3 %collective-permute-start.33 = (bf16[2,512,384]{1,2,0:T(8,128)(2,1)}, bf16[2,512,384]{1,2,0:T(8,128)(2,1)}, u32[]{:S(2)}, u32[]{:S(2)}) collective-permute-start(bf16[2,512,384]{1,2,0:T(8,128)(2,1)} %pad_maximum_fusion.3), channel_id=1, source_target_pairs={{0,1},{3,2},{4,5},{7,6},{8,9},{11,10},{12,13},{15,14},{16,17},{19,... | collective-permute-start | bytes 2359304 | tf_op jit(solution)/shard_map/ppermute | solution.py:197
  455.4 11.7 %all-to-all-start.1 = ((bf16[8,64,384]{2,1,0:T(8,128)(2,1)}), bf16[8,64,384]{2,1,0:T(8,128)(2,1)S(1)}, u32[]{:S(2)}, u32[]{:S(2)}) async-start(bf16[8,64,384]{2,1,0:T(8,128)(2,1)} %all_to_all.19), calls=%async_computation.1 | async-start | bytes 786432 | tf_op jit(solution)/shard_map/all_to_all | solution.py:214
  468.9 11.3 %collective-permute-start.38 = (bf16[2,512,384]{1,2,0:T(8,128)(2,1)}, bf16[2,512,384]{1,2,0:T(8,128)(2,1)}, u32[]{:S(2)}, u32[]{:S(2)}) collective-permute-start(bf16[2,512,384]{1,2,0:T(8,128)(2,1)} %collective-permute-done.37), channel_id=1, source_target_pairs={{1,2},{2,1},{5,6},{6,5},{9,10},{10,9},{13,14},{14,13},{17,18},{18,... | collective-permute-start | bytes 2359304 | tf_op jit(solution)/shard_map/ppermute | solution.py:197
  470.5 13.6 %collective-permute-start.42 = (bf16[2,512,384]{1,2,0:T(8,128)(2,1)}, bf16[2,512,384]{1,2,0:T(8,128)(2,1)}, u32[]{:S(2)}, u32[]{:S(2)}) collective-permute-start(bf16[2,512,384]{1,2,0:T(8,128)(2,1)} %collective-permute-done.41), channel_id=1, source_target_pairs={{1,2},{2,1},{5,6},{6,5},{9,10},{10,9},{13,14},{14,13},{17,18},{18,... | collective-permute-start | bytes 2359304 | tf_op jit(solution)/shard_map/ppermute | solution.py:197
  474.0 16.4 %collective-permute-start.34 = (bf16[2,512,384]{1,2,0:T(8,128)(2,1)}, bf16[2,512,384]{1,2,0:T(8,128)(2,1)}, u32[]{:S(2)}, u32[]{:S(2)}) collective-permute-start(bf16[2,512,384]{1,2,0:T(8,128)(2,1)} %collective-permute-done.33), channel_id=1, source_target_pairs={{1,2},{2,1},{5,6},{6,5},{9,10},{10,9},{13,14},{14,13},{17,18},{18,... | collective-permute-start | bytes 2359304 | tf_op jit(solution)/shard_map/ppermute | solution.py:197
  480.2 29.3 %collective-permute-start.39 = (bf16[2,512,384]{1,2,0:T(8,128)(2,1)}, bf16[2,512,384]{1,2,0:T(8,128)(2,1)}, u32[]{:S(2)}, u32[]{:S(2)}) collective-permute-start(bf16[2,512,384]{1,2,0:T(8,128)(2,1)} %collective-permute-done.38), channel_id=1, source_target_pairs={{2,3},{1,0},{6,7},{5,4},{10,11},{9,8},{14,15},{13,12},{18,19},{17,... | collective-permute-start | bytes 2359304 | tf_op jit(solution)/shard_map/ppermute | solution.py:197
  484.1 42.3 %collective-permute-start.43 = (bf16[2,512,384]{1,2,0:T(8,128)(2,1)}, bf16[2,512,384]{1,2,0:T(8,128)(2,1)}, u32[]{:S(2)}, u32[]{:S(2)}) collective-permute-start(bf16[2,512,384]{1,2,0:T(8,128)(2,1)} %collective-permute-done.42), channel_id=1, source_target_pairs={{2,3},{1,0},{6,7},{5,4},{10,11},{9,8},{14,15},{13,12},{18,19},{17,... | collective-permute-start | bytes 2359304 | tf_op jit(solution)/shard_map/ppermute | solution.py:197
  490.5 52.7 %collective-permute-start.35 = (bf16[2,512,384]{1,2,0:T(8,128)(2,1)}, bf16[2,512,384]{1,2,0:T(8,128)(2,1)}, u32[]{:S(2)}, u32[]{:S(2)}) collective-permute-start(bf16[2,512,384]{1,2,0:T(8,128)(2,1)} %collective-permute-done.34), channel_id=1, source_target_pairs={{2,3},{1,0},{6,7},{5,4},{10,11},{9,8},{14,15},{13,12},{18,19},{17,... | collective-permute-start | bytes 2359304 | tf_op jit(solution)/shard_map/ppermute | solution.py:197
  533.6 31.4 %collective-permute-start.40 = (bf16[640,3,1,128]{0,3,2,1:T(8,128)(2,1)}, bf16[640,3,1,128]{0,3,2,1:T(8,128)(2,1)S(1)}, u32[]{:S(2)}, u32[]{:S(2)}) collective-permute-start(bf16[640,3,1,128]{0,3,2,1:T(8,128)(2,1)} %bitcast.73), channel_id=1, source_target_pairs={{0,16},{16,0},{1,17},{17,1},{2,18},{18,2},{3,19},{19,3},{4,20},{20... | collective-permute-start | bytes 1474568 | tf_op jit(solution)/shard_map/ppermute | solution.py:204
  549.7 15.1 %collective-permute-start.36 = (bf16[640,3,1,128]{0,3,2,1:T(8,128)(2,1)S(1)}, bf16[640,3,1,128]{0,3,2,1:T(8,128)(2,1)S(1)}, u32[]{:S(2)}, u32[]{:S(2)}) collective-permute-start(bf16[640,3,1,128]{0,3,2,1:T(8,128)(2,1)S(1)} %bitcast.249), channel_id=1, source_target_pairs={{0,16},{16,0},{1,17},{17,1},{2,18},{18,2},{3,19},{19,3},{4,20},{20... | collective-permute-start | bytes 1474568 | tf_op jit(solution)/shard_map/ppermute | solution.py:204
  554.1 18.6 %collective-permute-start.44 = (bf16[640,3,1,128]{0,3,2,1:T(8,128)(2,1)S(1)}, bf16[640,3,1,128]{0,3,2,1:T(8,128)(2,1)S(1)}, u32[]{:S(2)}, u32[]{:S(2)}) collective-permute-start(bf16[640,3,1,128]{0,3,2,1:T(8,128)(2,1)S(1)} %bitcast.248), channel_id=1, source_target_pairs={{0,16},{16,0},{1,17},{17,1},{2,18},{18,2},{3,19},{19,3},{4,20},{20... | collective-permute-start | bytes 1474568 | tf_op jit(solution)/shard_map/ppermute | solution.py:204
  (33 other events, 132.8 us)
